TPU v7x, 32 devices: a whole 2x2x4 slice. The times are simulated.
32 devices in a mesh: seq: 4 (over z), vocab: 8 (over y, x, core).
Axes of the slice: x: 2, y: 2, z: 4, core: 2. Of those that a mesh axis runs over, the one named last changes fastest.
Arguments:
- hidden: bfloat16 [2048, 5376], P('seq', 'vocab'), may hold values from -64 to 64
- embed_cotangent: bfloat16 [2048, 5376], P('seq', 'vocab'), may hold values from -24 to 24
- table: bfloat16 [6144, 5376], P('vocab'), may hold values from -3 to 3
- token_ids: int32 [2048], P('seq'), may hold values from 0 to 6143
- target_ids: int32 [2048], P('seq'), may hold values from 0 to 6143
- loss_scale: float32 [2048], P('seq'), may hold values from 8 to 32
Outputs:
- grad_hidden: bfloat16 [2048, 5376], P('seq', 'vocab')
- grad_table: float32 [6144, 5376], P('vocab', 'seq')
- token_loss: float32 [2048], P('seq')
All inputs are finite; a program needn't handle non-finite values.
Results may differ from a plain program's by a relative error of at most 0.0047.
Values may be sent and summed in bfloat16 or wider, within the bound.
A program may use at most 192 MiB of HBM per device.

v0:
```python
import jax
import jax.numpy as jnp
from jax import lax
from jax.sharding import PartitionSpec as P


def body(hidden, embed_cotangent, table, token_ids, target_ids, loss_scale):
    rows_full, cotangent_full = (
        lax.all_gather(hidden, "vocab", axis=1, tiled=True),
        lax.all_gather(embed_cotangent, "vocab", axis=1, tiled=True),
    )
    vocab_rows = table.shape[0]
    vocab_base = lax.axis_index("vocab") * vocab_rows
    columns = vocab_base + jnp.arange(vocab_rows, dtype=jnp.int32)
    logits = lax.dot_general(
        rows_full, table, (((1,), (1,)), ((), ())), preferred_element_type=jnp.float32
    )
    target_hot = (target_ids[:, None] == columns[None, :]).astype(jnp.float32)
    target_local = jnp.sum(logits * target_hot, axis=1)
    row_top = lax.pmax(jnp.max(logits, axis=1), "vocab")
    local_total = jnp.sum(jnp.exp(logits - row_top[:, None]), axis=1)
    exp_total, target_logit = lax.psum((local_total, target_local), "vocab")
    log_norm = row_top + jnp.log(exp_total)
    token_loss = log_norm - target_logit
    probability = jnp.exp(logits - log_norm[:, None])
    logit_grad = (loss_scale[:, None] * (probability - target_hot)).astype(jnp.bfloat16)
    hidden_term = jnp.dot(logit_grad, table, preferred_element_type=jnp.float32)
    grad_hidden = lax.psum_scatter(hidden_term, "vocab", scatter_dimension=1, tiled=True).astype(
        jnp.bfloat16
    )
    contract_rows = (((0,), (0,)), ((), ()))
    token_hot = (token_ids[:, None] == columns[None, :]).astype(jnp.bfloat16)
    table_term = lax.dot_general(
        logit_grad, rows_full, contract_rows, preferred_element_type=jnp.float32
    )
    table_term = table_term + lax.dot_general(
        token_hot, cotangent_full, contract_rows, preferred_element_type=jnp.float32
    )
    grad_table = lax.psum_scatter(table_term, "seq", scatter_dimension=1, tiled=True)
    return (grad_hidden, grad_table, token_loss)


def solution(mesh):
    placed = (P("seq", "vocab"), P("seq", "vocab"), P("vocab", None), P("seq"), P("seq"), P("seq"))
    return jax.shard_map(
        body,
        mesh=mesh,
        in_specs=placed,
        out_specs=(P("seq", "vocab"), P("vocab", "seq"), P("seq")),
        check_vma=False,
    )
```

profile of v0, /device:TPU:13, one launch (start us, length us, event | category | flops | bytes accessed | tf_op | source)
XLA Modules:
  0.0 468.6 jit_solution(2721960368921387577)
XLA Ops:
  7.2 0.0 all-gather.3.cloned.1.call-start
  7.2 0.7 all-gather.3.cloned.1.call-update
  7.9 0.0 all-gather.5.cloned.1.call-start
  7.9 0.7 all-gather.5.cloned.1.call-update
  8.6 0.0 reduce-scatter.3.cloned.1.call-start
  8.7 0.0 copy-start.1
  8.7 44.7 %all-gather.3.cloned.1.call-done = bf16[512,5376]{0,1:T(8,128)(2,1)} async-done(((bf16[512,672]{0,1:T(8,128)(2,1)}), bf16[512,5376]{0,1:T(8,128)(2,1)}) %all-gather.3.cloned.1.call-update) | async-done | bytes 5505040 | tf_op jit(solution)/shard_map/all_gather | solution.py:9
  53.4 8.9 %fusion.12 = (f32[512]{0:T(512)S(1)}, f32[512,768]{1,0:T(8,128)S(1)}) fusion(bf16[512,5376]{0,1:T(8,128)(2,1)} %all-gather.3.cloned.1.call-done, bf16[768,5376]{1,0:T(8,128)(2,1)} %param.8), kind=kOutput, calls=%fused_computation.16 | convolution fusion | flops 4228251136 | bytes 15337472 | tf_op jit(solution)/shard_map/dot_general | solution.py:15
  62.4 0.0 copy-start.2
  62.4 11.7 %pmax.7 = f32[512]{0:T(512)S(1)} all-reduce(f32[512]{0:T(512)S(1)} %get-tuple-element.9), channel_id=1, replica_groups=mesh['seq'=4,'vocab'=8] {'vocab'}, use_global_device_ids=true, to_apply=%region_1.0 | all-reduce | flops 512 | bytes 4096 | tf_op jit(solution)/shard_map/pmax | solution.py:20
  74.1 0.0 copy-done.1
  74.1 0.6 fusion.3
  74.6 13.6 %all-reduce = (f32[512]{0:T(512)S(1)}, f32[512]{0:T(512)S(1)}) all-reduce(f32[512]{0:T(512)S(1)} %get-tuple-element.4, f32[512]{0:T(512)S(1)} %get-tuple-element.3), channel_id=1, replica_groups=mesh['seq'=4,'vocab'=8] {'vocab'}, use_global_device_ids=true, to_apply=%region_3.0 | all-reduce | flops 1024 | bytes 8192 | tf_op jit(solution)/shard_map/psum | solution.py:22
  88.3 0.6 fusion.11
  88.8 13.0 %fusion.9 = f32[512,5376]{0,1:T(8,128)} fusion(bf16[768,5376]{1,0:T(8,128)(2,1)} %param.8, f32[512,768]{1,0:T(8,128)S(1)} %get-tuple-element.10, s32[768]{0:T(1024)S(1)} %iota_add_fusion, f32[512]{0:T(512)S(1)} %get-tuple-element.8, f32[512]{0:T(512)S(1)} %copy-done.2, s32[512]{0:T(512)S(1)} %copy-done.1), kind=kOutput, calls=%fused_computation.14 | convolution fusion | flops 4230217728 | bytes 20849664 | tf_op jit(solution)/shard_map/dot_general | solution.py:27
  101.8 0.0 reduce-scatter.3.cloned.1.call-update
  101.9 0.0 copy-start
  101.9 0.0 reduce-scatter.5.cloned.1.call-start
  101.9 13.0 %fusion.7 = f32[768,5376]{0,1:T(8,128)} fusion(bf16[512,5376]{0,1:T(8,128)(2,1)} %all-gather.3.cloned.1.call-done, f32[512,768]{1,0:T(8,128)S(1)} %get-tuple-element.10, s32[768]{0:T(1024)S(1)} %iota_add_fusion, f32[512]{0:T(512)S(1)} %get-tuple-element.8, f32[512]{0:T(512)S(1)} %copy-done.2, s32[512]{0:T(512)S(1)} %copy-done.1), kind=kOutput, calls=%fused_computation.13 | convolution fusion | flops 4230217728 | bytes 23602176 | tf_op jit(solution)/shard_map/dot_general | solution.py:33
  114.9 18.5 %convolution_add_fusion = f32[768,5376]{0,1:T(8,128)} fusion(f32[768,5376]{0,1:T(8,128)} %fusion.7, bf16[512,5376]{0,1:T(8,128)(2,1)} %all-gather.5.cloned.1.call-done, s32[768]{0:T(1024)S(1)} %iota_add_fusion, s32[512]{0:T(512)S(1)} %copy-done), kind=kOutput, calls=%fused_computation | convolution fusion | flops 4232380416 | bytes 38540288 | tf_op jit(solution)/shard_map/dot_general | solution.py:36
  133.4 0.0 reduce-scatter.5.cloned.1.call-update
  133.5 52.4 %reduce-scatter.3.cloned.1.call-done = f32[512,672]{0,1:T(8,128)} async-done(((f32[512,5376]{0,1:T(8,128)}), f32[512,672]{0,1:T(8,128)}) %reduce-scatter.3.cloned.1.call-update) | async-done | bytes 1376272 | tf_op jit(solution)/shard_map/reduce_scatter | solution.py:28
  185.9 2.3 convert_element_type.12
  188.1 273.9 %reduce-scatter.5.cloned.1.call-done = f32[768,1344]{0,1:T(8,128)} async-done(((f32[768,5376]{0,1:T(8,128)}), f32[768,1344]{0,1:T(8,128)}) %reduce-scatter.5.cloned.1.call-update) | async-done | bytes 4128784 | tf_op jit(solution)/shard_map/reduce_scatter | solution.py:39
  (4 shorter events, 0.0 us)
Async XLA Ops:
  7.2 46.3 %all-gather.3.cloned.1.call-start = ((), (), s32[]{:S(2)}) async-start(), calls=%async_computation.2 | async-start | bytes 6193152 | tf_op jit(solution)/shard_map/all_gather | solution.py:9
  7.9 107.0 %all-gather.5.cloned.1.call-start = ((), (), s32[]{:S(2)}) async-start(), calls=%async_computation.4 | async-start | bytes 6193152 | tf_op jit(solution)/shard_map/all_gather | solution.py:10
  8.6 177.2 %reduce-scatter.3.cloned.1.call-start = ((), (), s32[]{:S(2)}) async-start(), calls=%async_computation.3 | async-start | bytes 12386304 | tf_op jit(solution)/shard_map/reduce_scatter | solution.py:28
  8.7 65.4 %copy-start.1 = (s32[512]{0:T(512)S(1)}, s32[512]{0:T(512)}, u32[]{:S(2)}) copy-start(s32[512]{0:T(512)} %param.10) | copy-start | bytes 6148
  62.4 26.5 %copy-start.2 = (f32[512]{0:T(512)S(1)}, f32[512]{0:T(512)}, u32[]{:S(2)}) copy-start(f32[512]{0:T(512)} %param.11) | copy-start | bytes 6148
  101.9 13.0 %copy-start = (s32[512]{0:T(512)S(1)}, s32[512]{0:T(512)}, u32[]{:S(2)}) copy-start(s32[512]{0:T(512)} %param.9) | copy-start | bytes 6148
  101.9 360.2 %reduce-scatter.5.cloned.1.call-start = ((), (), s32[]{:S(2)}) async-start(), calls=%async_computation.5 | async-start | bytes 20643840 | tf_op jit(solution)/shard_map/reduce_scatter | solution.py:39
Sparse Core Ops, SparseCore 0:
  9.9 43.5 all-gather.2
  55.3 42.5 all-gather.4
  102.0 83.8 reduce-scatter.2
  188.7 273.3 reduce-scatter.4
where the time goes:
time: 473 us; the launch traced here: 469 us
  waiting for transfers between devices  372 us (79%)
  matrix products  53.4 us (11%)
  blocking collectives  25.3 us (5%)
  between operations  13.8 us (3%)
    reduce_scatter x1, waiting for transfers between devices, body(): lax.psum_scatter(table_term, 'seq', scatter_dimension=1, tiled=True)  274 us
    reduce_scatter x1, waiting for transfers between devices, body(): lax.psum_scatter(hidden_term, 'vocab', scatter_dimension=1, tiled=True)  52.4 us
    all_gather x1, waiting for transfers between devices, body(): lax.all_gather(hidden, 'vocab', axis=1, tiled=True)  44.7 us
    dot_general x1, matrix products, body(): lax.dot_general(token_hot, cotangent_full, contract_rows, preferred_eleme...  18.5 us
    psum x1, blocking collectives, body(): exp_total, target_logit = lax.psum((local_total, target_local), 'vocab')  13.6 us
    dot_general x1, matrix products, body(): hidden_term = jnp.dot(logit_grad, table, preferred_element_type=jnp.float32)  13 us
    dot_general x1, matrix products, body(): lax.dot_general(logit_grad, rows_full, contract_rows, preferred_element_t...  13 us
    pmax x1, blocking collectives, body(): row_top = lax.pmax(jnp.max(logits, axis=1), 'vocab')  11.7 us
  transfers between devices with their start and end apart: 4, of which 3 were waited for; matrix products, arithmetic and copies ran while one was open for 12% of the time, Pallas kernels for 0%

commit v1 on v0

v1 whole, which is shorter than its diff:
```python
import jax
import jax.numpy as jnp
from jax import lax
from jax.sharding import PartitionSpec as P


def body(hidden, embed_cotangent, table, token_ids, target_ids, loss_scale):
    n_seq, n_vocab = lax.axis_size("seq"), lax.axis_size("vocab")
    per = n_vocab // n_seq
    vocab_rows = table.shape[0]
    vocab_base = lax.axis_index("vocab") * vocab_rows
    columns = vocab_base + jnp.arange(vocab_rows, dtype=jnp.int32)
    rows_full = lax.all_gather(hidden, "vocab", axis=1, tiled=True)
    swap = [
        (s * n_vocab + c * per + r, c * n_vocab + s * per + r)
        for s in range(n_seq)
        for c in range(n_seq)
        for r in range(per)
    ]
    hidden_cols = lax.all_gather(lax.ppermute(hidden, ("seq", "vocab"), swap), "vocab", axis=0)
    cot_cols = lax.all_gather(
        lax.ppermute(embed_cotangent, ("seq", "vocab"), swap), "vocab", axis=0
    )
    ids_all = lax.all_gather(token_ids, "seq", axis=0, tiled=True)
    logits = lax.dot_general(
        rows_full, table, (((1,), (1,)), ((), ())), preferred_element_type=jnp.float32
    )
    target_hot = (target_ids[:, None] == columns[None, :]).astype(jnp.float32)
    own_top = jnp.max(logits, axis=1)
    own_total = jnp.sum(jnp.exp(logits - own_top[:, None]), axis=1)
    own_target = jnp.sum(logits * target_hot, axis=1)
    stats = lax.all_gather(jnp.stack([own_top, own_total, own_target]), "vocab", axis=0)
    row_top = jnp.max(stats[:, 0], axis=0)
    exp_total = jnp.sum(stats[:, 1] * jnp.exp(stats[:, 0] - row_top), axis=0)
    log_norm = row_top + jnp.log(exp_total)
    token_loss = log_norm - jnp.sum(stats[:, 2], axis=0)
    probability = jnp.exp(logits - log_norm[:, None])
    logit_grad = (loss_scale[:, None] * (probability - target_hot)).astype(jnp.bfloat16)
    grad_all = lax.all_gather(logit_grad, "seq", axis=0)
    hidden_term = jnp.dot(logit_grad, table, preferred_element_type=jnp.float32)
    grad_hidden = lax.psum_scatter(
        hidden_term.astype(jnp.bfloat16), "vocab", scatter_dimension=1, tiled=True
    )
    rows, cols = hidden.shape

    def columns_of(blocks):
        blocks = blocks.reshape(n_seq, per, rows, cols).transpose(0, 2, 1, 3)
        return blocks.reshape(n_seq * rows, per * cols)

    contract_rows = (((0,), (0,)), ((), ()))
    token_hot = (ids_all[:, None] == columns[None, :]).astype(jnp.bfloat16)
    grad_table = lax.dot_general(
        token_hot, columns_of(cot_cols), contract_rows, preferred_element_type=jnp.float32
    ) + lax.dot_general(
        grad_all.reshape(n_seq * rows, vocab_rows),
        columns_of(hidden_cols),
        contract_rows,
        preferred_element_type=jnp.float32,
    )
    return (grad_hidden, grad_table, token_loss)


def solution(mesh):
    placed = (P("seq", "vocab"), P("seq", "vocab"), P("vocab", None), P("seq"), P("seq"), P("seq"))
    return jax.shard_map(
        body,
        mesh=mesh,
        in_specs=placed,
        out_specs=(P("seq", "vocab"), P("vocab", "seq"), P("seq")),
        check_vma=False,
    )
```

time: 473 us -> 321 us (0.68)
  waiting for transfers between devices: 372 us -> 166 us
  local copies, waits for them, and re-layouts: 0.02 us -> 48.1 us
  blocking collectives: 25.3 us -> 44.7 us
  matrix products: 53.4 us -> 34 us
  starting transfers between devices: 0.16 us -> 9.35 us
    reduce_scatter x2 -> x1, waiting for transfers between devices: 326 us -> 48.2 us  [body(): lax.psum_scatter(hidden_term.astype(jnp.bfloat16), 'vocab', scatter_dimen...]
    ppermute x0 -> x2, waiting for transfers between devices: none -> 60.3 us  [the longest x1 31 us: body(): lax.ppermute(hidden, ('seq', 'vocab'), swap)]
    all_gather x0 -> x2, blocking collectives: none -> 44.7 us  [the longest x1 34.1 us: body(): lax.all_gather(jnp.stack([own_top, own_total, own_target]), 'vocab', axis=0)]
    reshape x0 -> x4, local copies, waits for them, and re-layouts: none -> 36.2 us  [columns_of(): blocks = blocks.reshape(n_seq, per, rows, cols).transpose(0, 2, 1, 3)]
    dot_general x2, matrix products: 31.5 us -> 14.5 us  [the longest x1 7.48 us: body(): lax.dot_general(grad_all.reshape(n_seq * rows, vocab_rows), columns_of(hi...]
    psum x1 -> x0, blocking collectives: 13.6 us -> none  [body(): exp_total, target_logit = lax.psum((local_total, target_local), 'vocab')]
    unnamed x6 -> x14, local copies, waits for them, and re-layouts: 0.02 us -> 12 us
    pmax x1 -> x0, blocking collectives: 11.7 us -> none  [body(): row_top = lax.pmax(jnp.max(logits, axis=1), 'vocab')]
  transfers between devices with their start and end apart: 4 -> 7, of which waited for: 3 -> 6; matrix products, arithmetic and copies ran while one was open for 12% -> 26% of each run, Pallas kernels for 0% -> 0%
where the time goes in v1:
time: 321 us; the launch traced here: 318 us
  waiting for transfers between devices  166 us (52%)
  local copies, waits for them, and re-layouts  48.1 us (15%)
  blocking collectives  44.7 us (14%)
  matrix products  34 us (11%)
  between operations  13.9 us (4%)
  starting transfers between devices  9.35 us (3%)
    reduce_scatter x1, waiting for transfers between devices, body(): lax.psum_scatter(hidden_term.astype(jnp.bfloat16), 'vocab', scatter_dimen...  48.2 us
    all_gather x1, waiting for transfers between devices, body(): grad_all = lax.all_gather(logit_grad, 'seq', axis=0)  40.8 us
    reshape x4, local copies, waits for them, and re-layouts, columns_of(): blocks = blocks.reshape(n_seq, per, rows, cols).transpose(0, 2, 1, 3)  36.2 us
    all_gather x1, blocking collectives, body(): lax.all_gather(jnp.stack([own_top, own_total, own_target]), 'vocab', axis=0)  34.1 us
    ppermute x1, waiting for transfers between devices, body(): lax.ppermute(hidden, ('seq', 'vocab'), swap)  31 us
    ppermute x1, waiting for transfers between devices, body(): lax.ppermute(embed_cotangent, ('seq', 'vocab'), swap)  29.3 us
    all_gather x1, waiting for transfers between devices, body(): lax.all_gather(lax.ppermute(embed_cotangent, ('seq', 'vocab'), swap), 'vo...  12.8 us
    unnamed x14, local copies, waits for them, and re-layouts  12 us
  transfers between devices with their start and end apart: 7, of which 6 were waited for; matrix products, arithmetic and copies ran while one was open for 26% of the time, Pallas kernels for 0%

profile of v1, /device:TPU:13, one launch (start us, length us, event | category | flops | bytes accessed | tf_op | source)
XLA Modules:
  0.0 318.1 jit_solution(16813075434385352548)
XLA Ops:
  7.2 0.7 all-gather.11.cloned.1.call-update
  7.9 4.1 %collective-permute-start.1 = (bf16[512,672]{0,1:T(8,128)(2,1)}, bf16[512,672]{0,1:T(8,128)(2,1)S(1)}, u32[]{:S(2)}, u32[]{:S(2)}) collective-permute-start(bf16[512,672]{0,1:T(8,128)(2,1)} %param.6), channel_id=1, source_target_pairs={{0,0},{1,1},{2,8},{3,9},{4,16},{5,17},{6,24},{7,25},{8,2},{9,3},{1... | collective-permute-start | bytes 2064392 | tf_op jit(solution)/shard_map/ppermute | solution.py:20
  12.0 31.0 %collective-permute-done.1 = bf16[512,672]{0,1:T(8,128)(2,1)S(1)} collective-permute-done((bf16[512,672]{0,1:T(8,128)(2,1)}, bf16[512,672]{0,1:T(8,128)(2,1)S(1)}, u32[]{:S(2)}, u32[]{:S(2)}) %collective-permute-start.1) | collective-permute-done | bytes 688160 | tf_op jit(solution)/shard_map/ppermute | solution.py:20
  43.0 0.9 copy-done.1
  44.0 5.1 %collective-permute-start = (bf16[512,672]{0,1:T(8,128)(2,1)}, bf16[512,672]{0,1:T(8,128)(2,1)S(1)}, u32[]{:S(2)}, u32[]{:S(2)}) collective-permute-start(bf16[512,672]{0,1:T(8,128)(2,1)} %param.7), channel_id=1, source_target_pairs={{0,0},{1,1},{2,8},{3,9},{4,16},{5,17},{6,24},{7,25},{8,2},{9,3},{1... | collective-permute-start | bytes 2064392 | tf_op jit(solution)/shard_map/ppermute | solution.py:22
  49.1 29.3 %collective-permute-done = bf16[512,672]{0,1:T(8,128)(2,1)S(1)} collective-permute-done((bf16[512,672]{0,1:T(8,128)(2,1)}, bf16[512,672]{0,1:T(8,128)(2,1)S(1)}, u32[]{:S(2)}, u32[]{:S(2)}) %collective-permute-start) | collective-permute-done | bytes 688160 | tf_op jit(solution)/shard_map/ppermute | solution.py:22
  78.4 0.9 copy-done.2
  79.4 2.7 all-gather.11.cloned.1.call-done
  82.1 8.9 %fusion.17 = (f32[512]{0:T(512)S(1)}, f32[512,768]{1,0:T(8,128)S(1)}) fusion(bf16[512,5376]{0,1:T(8,128)(2,1)} %all-gather.11.cloned.1.call-done, bf16[768,5376]{1,0:T(8,128)(2,1)} %param.8), kind=kOutput, calls=%fused_computation.25 | convolution fusion | flops 4228251136 | bytes 15337472 | tf_op jit(solution)/shard_map/dot_general | solution.py:25
  91.5 34.1 %all-gather.4 = f32[8,3,512]{2,1,0:T(4,128)S(1)} all-gather(f32[1,3,512]{2,1,0:T(4,128)S(1)} %maximum_bitcast_fusion), channel_id=2, replica_groups=mesh['seq'=4,'vocab'=8] {'vocab'}, dimensions={0}, use_global_device_ids=true | all-gather | bytes 55296 | tf_op jit(solution)/shard_map/all_gather | solution.py:32
  126.3 1.3 fusion.10
  127.7 10.6 %convolution_convert_fusion = bf16[512,5376]{0,1:T(8,128)(2,1)} fusion(bf16[512,768]{1,0:T(8,128)(2,1)} %fusion.10, bf16[768,5376]{1,0:T(8,128)(2,1)} %param.8), kind=kOutput, calls=%fused_computation | convolution fusion | flops 4230610944 | bytes 14548992 | tf_op jit(solution)/shard_map/dot_general | solution.py:40
  139.0 10.6 %all-gather.5 = s32[4,1,512]{2,1,0:T(1,128)S(1)} all-gather(s32[1,1,512]{2,1,0:T(1,128)S(1)} %bitcast.50), channel_id=1, replica_groups=mesh['seq'=4,'vocab'=8] {'seq'}, dimensions={0}, use_global_device_ids=true | all-gather | bytes 10240 | tf_op jit(solution)/shard_map/all_gather | solution.py:24
  149.6 13.4 %reshape.39 = bf16[4,2,512,672]{2,1,0,3:T(2,128)(2,1)} reshape(bf16[4096,672]{0,1:T(8,128)(2,1)} %all-gather.17.cloned.1.call-done) | data formatting | bytes 11010048 | tf_op jit(solution)/shard_map/reshape | solution.py:47
  163.0 4.7 %copy.15 = bf16[4,2,512,672]{2,0,3,1:T(4,128)(2,1)S(1)} copy(bf16[4,2,512,672]{2,1,0,3:T(2,128)(2,1)} %reshape.39) | data formatting | bytes 11010048 | tf_op jit(solution)/shard_map/reshape | solution.py:47
  167.7 4.7 %copy.20 = bf16[168,8,4,512]{3,1,2,0:T(8,128)(2,1)} copy(bf16[168,8,4,512]{3,2,1,0:T(4,128)(2,1)S(1)} %bitcast.42) | data formatting | bytes 11010048
  172.4 12.8 %all-gather.13.cloned.1.call-done = bf16[4096,672]{0,1:T(8,128)(2,1)} async-done(((bf16[512,672]{0,1:T(8,128)(2,1)}), bf16[4096,672]{0,1:T(8,128)(2,1)}) %all-gather.13.cloned.1.call-update) | async-done | bytes 5505040 | tf_op jit(solution)/shard_map/all_gather | solution.py:21
  185.2 13.4 %reshape.36 = bf16[4,2,512,672]{2,1,0,3:T(2,128)(2,1)} reshape(bf16[4096,672]{0,1:T(8,128)(2,1)} %all-gather.13.cloned.1.call-done) | data formatting | bytes 11010048 | tf_op jit(solution)/shard_map/reshape | solution.py:47
  198.6 4.7 %copy.14 = bf16[4,2,512,672]{2,0,3,1:T(4,128)(2,1)S(1)} copy(bf16[4,2,512,672]{2,1,0,3:T(2,128)(2,1)} %reshape.36) | data formatting | bytes 11010048 | tf_op jit(solution)/shard_map/reshape | solution.py:47
  203.3 4.8 %copy.19 = bf16[168,8,4,512]{3,1,2,0:T(8,128)(2,1)} copy(bf16[168,8,4,512]{3,2,1,0:T(4,128)(2,1)S(1)} %bitcast.43) | data formatting | bytes 11010048
  208.1 40.8 %all-gather.15.cloned.1.call-done = bf16[2048,768]{1,0:T(8,128)(2,1)} async-done(((bf16[512,768]{1,0:T(8,128)(2,1)}), bf16[2048,768]{1,0:T(8,128)(2,1)}) %all-gather.15.cloned.1.call-update) | async-done | bytes 3145744 | tf_op jit(solution)/shard_map/all_gather | solution.py:39
  248.9 7.5 %fusion.18 = f32[768,1344]{0,1:T(8,128)S(1)} fusion(bf16[2048,1344]{0,1:T(8,128)(2,1)} %bitcast.44, bf16[2048,768]{1,0:T(8,128)(2,1)} %all-gather.15.cloned.1.call-done), kind=kOutput, calls=%fused_computation.26 | convolution fusion | flops 4227858432 | bytes 12779520 | tf_op jit(solution)/shard_map/dot_general | solution.py:54
  256.4 7.0 %fusion.2 = f32[768,1344]{0,1:T(8,128)} fusion(f32[768,1344]{0,1:T(8,128)S(1)} %fusion.18, bf16[2048,1344]{0,1:T(8,128)(2,1)S(1)} %bitcast.45, s32[768]{0:T(1024)S(1)} %iota_add_fusion, s32[2048]{0:T(1024)S(1)} %bitcast.49), kind=kOutput, calls=%fused_computation.3 | convolution fusion | flops 4230463488 | bytes 13773824 | tf_op jit(solution)/shard_map/dot_general | solution.py:52
  263.4 48.2 %reduce-scatter.2.cloned.1.call-done = bf16[512,672]{0,1:T(8,128)(2,1)} async-done(((bf16[512,5376]{0,1:T(8,128)(2,1)}), bf16[512,672]{0,1:T(8,128)(2,1)}) %reduce-scatter.2.cloned.1.call-update) | async-done | bytes 688144 | tf_op jit(solution)/shard_map/reduce_scatter | solution.py:41
  (26 shorter events, 2.2 us)
Async XLA Ops:
  7.2 74.9 %all-gather.11.cloned.1.call-start = ((), (), s32[]{:S(2)}) async-start(), calls=%async_computation.1 | async-start | bytes 6193152 | tf_op jit(solution)/shard_map/all_gather | solution.py:13
  7.9 141.7 %all-gather.17.cloned.1.call-start = ((), (), s32[]{:S(2)}) async-start(), calls=%async_computation.5 | async-start | bytes 6193152 | tf_op jit(solution)/shard_map/all_gather | solution.py:20
  7.9 35.1 %collective-permute-start.1 = (bf16[512,672]{0,1:T(8,128)(2,1)}, bf16[512,672]{0,1:T(8,128)(2,1)S(1)}, u32[]{:S(2)}, u32[]{:S(2)}) collective-permute-start(bf16[512,672]{0,1:T(8,128)(2,1)} %param.6), channel_id=1, source_target_pairs={{0,0},{1,1},{2,8},{3,9},{4,16},{5,17},{6,24},{7,25},{8,2},{9,3},{1... | collective-permute-start | bytes 2064392 | tf_op jit(solution)/shard_map/ppermute | solution.py:20
  43.0 0.9 copy-start.1
  43.9 141.3 %all-gather.13.cloned.1.call-start = ((), (), s32[]{:S(2)}) async-start(), calls=%async_computation.3 | async-start | bytes 6193152 | tf_op jit(solution)/shard_map/all_gather | solution.py:21
  44.0 34.4 %collective-permute-start = (bf16[512,672]{0,1:T(8,128)(2,1)}, bf16[512,672]{0,1:T(8,128)(2,1)S(1)}, u32[]{:S(2)}, u32[]{:S(2)}) collective-permute-start(bf16[512,672]{0,1:T(8,128)(2,1)} %param.7), channel_id=1, source_target_pairs={{0,0},{1,1},{2,8},{3,9},{4,16},{5,17},{6,24},{7,25},{8,2},{9,3},{1... | collective-permute-start | bytes 2064392 | tf_op jit(solution)/shard_map/ppermute | solution.py:22
  78.4 0.9 copy-start.2
  79.3 169.6 %all-gather.15.cloned.1.call-start = ((), (), s32[]{:S(2)}) async-start(), calls=%async_computation.4 | async-start | bytes 3932160 | tf_op jit(solution)/shard_map/all_gather | solution.py:39
  79.4 11.6 %copy-start.3 = (s32[512]{0:T(512)S(1)}, s32[512]{0:T(512)}, u32[]{:S(2)}) copy-start(s32[512]{0:T(512)} %param.10) | copy-start | bytes 6148
  79.4 46.9 %copy-start.5 = (f32[512]{0:T(512)S(1)}, f32[512]{0:T(512)}, u32[]{:S(2)}) copy-start(f32[512]{0:T(512)} %param.11) | copy-start | bytes 6148
  127.7 183.9 %reduce-scatter.2.cloned.1.call-start = ((), (), s32[]{:S(2)}) async-start(), calls=%async_computation.2 | async-start | bytes 6193152 | tf_op jit(solution)/shard_map/reduce_scatter | solution.py:41
  138.3 0.7 copy-start.4
  248.9 7.5 %copy-start = (bf16[168,8,4,512]{3,1,2,0:T(8,128)(2,1)S(1)}, bf16[168,8,4,512]{3,1,2,0:T(8,128)(2,1)}, u32[]{:S(2)}) copy-start(bf16[168,8,4,512]{3,1,2,0:T(8,128)(2,1)} %copy.19) | copy-start | bytes 16515076
Sparse Core Ops, SparseCore 0:
  9.9 72.1 all-gather.10
  83.9 55.9 all-gather.16
  141.8 43.3 all-gather.12
  187.2 61.6 all-gather.14
  252.7 58.7 reduce-scatter.1

commit v2 on v0

v2 whole, which is shorter than its diff:
```python
import functools

import jax
import jax.numpy as jnp
from jax import lax
from jax.experimental import pallas as pl
from jax.experimental.pallas import tpu as pltpu
from jax.sharding import PartitionSpec as P

MESH = pl.DeviceIdType.MESH
F32 = jnp.float32
BF16 = jnp.bfloat16
CORES = 2
CHUNK = 128


def dot(a, b, dims=(((1,), (0,)), ((), ()))):
    return lax.dot_general(a, b, dims, preferred_element_type=F32)


def kernel(
    n_seq, n_vocab,
    hid, cot, table, ids, target, scale,
    gh, gt, loss,
    raw, tab, rows, hcols, ccols, grads, logits, sends, sib, shares, own, stats, ids_all, norm,
    table_sem, local_sem, push_sem, fwd_sem, block_sem, swap_sem, stat_send, stat_recv, ids_send, ids_recv,
    up_sem, down_sem, grads_recv, sib_send, sib_recv, share_send, share_recv,
):
    per = n_vocab // n_seq
    chips = n_vocab // CORES
    cols, tokens = hid.shape
    vocab_rows, _ = table.shape
    s, v = lax.axis_index("seq"), lax.axis_index("vocab")
    c, k = v // CORES, v % CORES
    twin = c * CORES + (1 - k)
    swap_to, swap_slot = v // per, s * per + v % per
    is_self = swap_to == s
    base = v * vocab_rows

    def remote(src, dst, send, recv, where):
        return pltpu.make_async_remote_copy(
            src_ref=src, dst_ref=dst, send_sem=send, recv_sem=recv,
            device_id=where, device_id_type=MESH,
        )

    def loop(lo, hi, fn):
        lax.fori_loop(lo, hi, lambda i, z: (fn(i), z)[1], 0)

    def fetch(i):
        at = pl.ds(pl.multiple_of(i * CHUNK, CHUNK), CHUNK)
        return pltpu.make_async_copy(table.at[at], raw.at[i % 2], table_sem.at[i % 2])
    fetch(0).start()
    keep = pltpu.make_async_copy(hid, rows.at[v], local_sem)
    keep.start()

    barrier = pltpu.get_barrier_semaphore()
    loop(1, n_vocab, lambda i: pl.semaphore_signal(
        barrier, inc=1, device_id=(s, (v + i) % n_vocab), device_id_type=MESH))
    loop(1, n_seq, lambda i: pl.semaphore_signal(
        barrier, inc=1, device_id=((s + i) % n_seq, v), device_id_type=MESH))

    @pl.when(jnp.logical_not(is_self))
    def _():
        pl.semaphore_signal(barrier, inc=1, device_id=(swap_to, swap_slot), device_id_type=MESH)

    pl.semaphore_wait(barrier, n_vocab + n_seq - 2 + jnp.where(is_self, 0, 1))

    def push(a, src, buf):
        def one(i):
            return remote(src, buf.at[v], push_sem.at[a, i], block_sem.at[a, v],
                          (s, ((c + i) % chips) * CORES + k))
        loop(1, chips, lambda i: one(i).start())
        remote(src, buf.at[v], push_sem.at[a, 0], block_sem.at[a, v], (s, twin)).start()

    def push_done(a, src, buf):
        def one(i):
            remote(src, buf.at[v], push_sem.at[a, i], block_sem.at[a, v], (s, twin)).wait_send()
        loop(0, chips, one)

    def arrived(a, buf, u):
        remote(buf.at[u], buf.at[u], fwd_sem.at[a, 0], block_sem.at[a, u], (s, twin)).wait_recv()

    def forward(a, buf, i):
        u = ((c + i) % chips) * CORES + k
        return remote(buf.at[u], buf.at[u], fwd_sem.at[a, i], block_sem.at[a, u], (s, twin))

    push(0, hid, rows)

    for a, src, buf in ((1, hid, hcols), (2, cot, ccols)):
        @pl.when(is_self)
        def _(a=a, src=src, buf=buf):
            stay = pltpu.make_async_copy(src, buf.at[v], swap_sem.at[a])
            stay.start()
            stay.wait()

        @pl.when(jnp.logical_not(is_self))
        def _(a=a, src=src, buf=buf):
            remote(src, buf.at[swap_slot], swap_sem.at[a], block_sem.at[a, swap_slot],
                   (swap_to, swap_slot)).start()

    ids_all[s] = ids[...]

    def send_ids(i):
        remote(ids, ids_all.at[s], ids_send.at[i], ids_recv.at[s], ((s + i) % n_seq, v)).start()
    loop(1, n_seq, send_ids)

    pieces = vocab_rows // CHUNK

    def split(i):
        @pl.when(i + 1 < pieces)
        def _():
            fetch(i + 1).start()
        fetch(i).wait()
        at = pl.ds(pl.multiple_of(i * CHUNK, CHUNK), CHUNK)
        for u in range(n_vocab):
            tab[u, at, :] = raw[i % 2, :, u * cols:(u + 1) * cols]
    loop(0, pieces, split)

    logits[...] = jnp.zeros_like(logits)
    gt[...] = jnp.zeros_like(gt)
    keep.wait()

    def add_logits(u):
        logits[...] += dot(tab[u], rows[u])

    def logit_step(i):
        ci = (c + i) % chips

        @pl.when(i > 0)
        def _():
            arrived(0, rows, ci * CORES + k)
            forward(0, rows, i).start()
        add_logits(ci * CORES + k)
        arrived(0, rows, ci * CORES + 1 - k)
        add_logits(ci * CORES + 1 - k)
    loop(0, chips, logit_step)

    @pl.when(jnp.logical_not(is_self))
    def _():
        arrived(1, hcols, v)
        arrived(2, ccols, v)
    push(1, hcols.at[v], hcols)

    def piece(i):
        at = pl.ds(pl.multiple_of(i * CHUNK, CHUNK), CHUNK)
        entry = base + i * CHUNK + lax.broadcasted_iota(jnp.int32, (CHUNK, tokens), 0)
        return at, entry

    top = lax.fori_loop(
        0, pieces,
        lambda i, m: jnp.maximum(m, jnp.max(logits[piece(i)[0], :], axis=0, keepdims=True)),
        jnp.full((1, tokens), -jnp.inf, F32))

    def sums(i, carry):
        total, picked = carry
        at, entry = piece(i)
        x = logits[at, :]
        total += jnp.sum(jnp.exp(x - top), axis=0, keepdims=True)
        picked += jnp.sum(jnp.where(entry == target[...], x, 0.0), axis=0, keepdims=True)
        return total, picked
    zero = jnp.zeros((1, tokens), F32)
    total, picked = lax.fori_loop(0, pieces, sums, (zero, zero))
    stats[v] = jnp.concatenate([top, total, picked, jnp.zeros((5, tokens), F32)], axis=0)

    def stat(i):
        return remote(stats.at[v], stats.at[v], stat_send.at[i], stat_recv.at[v],
                      (s, (v + i) % n_vocab))
    loop(1, n_vocab, lambda i: stat(i).start())

    def stat_wait(i):
        u = (v + i) % n_vocab
        remote(stats.at[u], stats.at[u], stat_send.at[i], stat_recv.at[u], (s, twin)).wait_recv()
    loop(1, n_vocab, stat_wait)
    every = stats[...]
    row_top = jnp.max(every[:, 0, :], axis=0, keepdims=True)
    exp_total = jnp.sum(every[:, 1, :] * jnp.exp(every[:, 0, :] - row_top), axis=0, keepdims=True)
    log_norm = row_top + jnp.log(exp_total)
    loss[...] = log_norm - jnp.sum(every[:, 2, :], axis=0, keepdims=True)
    norm[...] = log_norm

    def logit_grad(i):
        at, entry = piece(i)
        hot = jnp.where(entry == target[...], 1.0, 0.0)
        g = scale[...] * (jnp.exp(logits[at, :] - norm[...]) - hot)
        grads[s, :, at] = g.T.astype(BF16)
    loop(0, pieces, logit_grad)

    def go_up(b):
        return remote(grads.at[b], grads.at[b], up_sem.at[b], grads_recv.at[b],
                      (jnp.minimum(s + 1, n_seq - 1), v))

    def go_down(b):
        return remote(grads.at[b], grads.at[b], down_sem.at[b], grads_recv.at[b],
                      (jnp.maximum(s - 1, 0), v))

    @pl.when(s < n_seq - 1)
    def _():
        go_up(s).start()

    @pl.when(s > 0)
    def _():
        go_down(s).start()

    def sib_copy(ci):
        slot = sends.at[ci * CORES + 1 - k]
        return remote(slot, sib.at[ci], sib_send.at[ci], sib_recv.at[ci], (s, twin))

    def to_twin(i):
        ci = (c + i) % chips
        u = ci * CORES + 1 - k
        sends[u] = dot(grads[s], tab[u]).astype(BF16)
        sib_copy(ci).start()
    loop(1, chips + 1, to_twin)

    def share_copy(ci):
        slot = sends.at[ci * CORES + k]
        return remote(slot, shares.at[c], share_send.at[ci], share_recv.at[c], (s, ci * CORES + k))

    def to_chips(i):
        ci = (c + i) % chips
        u = ci * CORES + k
        own[...] = dot(grads[s], tab[u])
        sib_copy(ci).wait_recv()
        own[...] += sib[ci].astype(F32)

        @pl.when(i < chips)
        def _():
            sends[u] = own[...].astype(BF16)
            share_copy(ci).start()
    loop(1, chips + 1, to_chips)
    push(2, ccols.at[v], ccols)

    def add_head(b):
        def one(r):
            gt[r] += dot(hcols[b * per + r], grads[b])
        loop(0, per, one)

    def take_grads(j):
        @pl.when(s >= j)
        def _():
            b = s - j
            go_up(b).wait_recv()

            @pl.when(s < n_seq - 1)
            def _():
                go_up(b).start()

        @pl.when(s + j < n_seq)
        def _():
            b = s + j
            go_down(b).wait_recv()

            @pl.when(s > 0)
            def _():
                go_down(b).start()

    def add_heads(j):
        @pl.when(s >= j)
        def _():
            add_head(s - j)

        @pl.when(s + j < n_seq)
        def _():
            add_head(s + j)

    def relay(a, buf):
        def one(i):
            arrived(a, buf, ((c + i) % chips) * CORES + k)
            forward(a, buf, i).start()
        loop(1, chips, one)
        loop(0, chips, lambda i: arrived(a, buf, ((c + i) % chips) * CORES + 1 - k))

    take_grads(1)
    relay(1, hcols)
    add_head(s)
    add_heads(1)
    for j in range(2, n_seq):
        take_grads(j)
        add_heads(j)

    def ids_wait(i):
        b = (s + i) % n_seq
        remote(ids, ids_all.at[b], ids_send.at[i], ids_recv.at[b], ((s + i) % n_seq, v)).wait_recv()
    loop(1, n_seq, ids_wait)

    def share_add(i):
        ci = (c + i) % chips
        remote(shares.at[ci], shares.at[ci], share_send.at[ci], share_recv.at[ci],
               (s, twin)).wait_recv()
        own[...] += shares[ci].astype(F32)
    loop(1, chips, share_add)
    gh[...] = own[...].T.astype(BF16)

    relay(2, ccols)

    def add_embed(b):
        entry = base + lax.broadcasted_iota(jnp.int32, (vocab_rows, tokens), 0)
        hot = jnp.where(entry == ids_all[b][0:1, :], 1.0, 0.0).astype(BF16)

        def one(r):
            gt[r] += dot(ccols[b * per + r], hot, (((1,), (1,)), ((), ())))
        loop(0, per, one)
    loop(0, n_seq, add_embed)

    push_done(0, hid, rows)
    push_done(1, hcols.at[v], hcols)
    push_done(2, ccols.at[v], ccols)
    for a, buf in ((0, rows), (1, hcols), (2, ccols)):
        loop(1, chips, lambda i, a=a, buf=buf: forward(a, buf, i).wait_send())
    for a, src, buf in ((1, hid, hcols), (2, cot, ccols)):
        @pl.when(jnp.logical_not(is_self))
        def _(a=a, src=src, buf=buf):
            remote(src, buf.at[swap_slot], swap_sem.at[a], block_sem.at[a, swap_slot],
                   (swap_to, swap_slot)).wait_send()

    def ids_left(i):
        remote(ids, ids_all.at[s], ids_send.at[i], ids_recv.at[s], ((s + i) % n_seq, v)).wait_send()
    loop(1, n_seq, ids_left)
    loop(1, n_vocab, lambda i: stat(i).wait_send())
    loop(0, chips, lambda i: sib_copy(i).wait_send())
    loop(1, chips, lambda i: share_copy((c + i) % chips).wait_send())
    for b in range(n_seq):
        @pl.when(jnp.logical_and(s >= b, s < n_seq - 1))
        def _(b=b):
            go_up(b).wait_send()

        @pl.when(jnp.logical_and(s <= b, s > 0))
        def _(b=b):
            go_down(b).wait_send()


def body(hidden, embed_cotangent, table, token_ids, target_ids, loss_scale):
    n_seq, n_vocab = lax.axis_size("seq"), lax.axis_size("vocab")
    per, chips = n_vocab // n_seq, n_vocab // CORES
    tokens, cols = hidden.shape
    vocab_rows, width = table.shape
    vmem = pl.BlockSpec(memory_space=pltpu.VMEM)
    dma = pltpu.SemaphoreType.DMA
    blocks = pltpu.VMEM((n_vocab, cols, tokens), BF16)
    halves = pltpu.VMEM((chips, tokens, cols), BF16)
    gh, gt, loss = pl.pallas_call(
        functools.partial(kernel, n_seq, n_vocab),
        out_shape=(
            jax.ShapeDtypeStruct((cols, tokens), BF16),
            jax.ShapeDtypeStruct((per, cols, vocab_rows), F32),
            jax.ShapeDtypeStruct((1, tokens), F32),
        ),
        in_specs=[vmem, vmem, pl.BlockSpec(memory_space=pl.ANY), vmem, vmem, vmem],
        out_specs=(vmem, vmem, vmem),
        scratch_shapes=[
            pltpu.VMEM((2, CHUNK, width), BF16),
            pltpu.VMEM((n_vocab, vocab_rows, cols), BF16),
            blocks, blocks, blocks,
            pltpu.VMEM((n_seq, tokens, vocab_rows), BF16),
            pltpu.VMEM((vocab_rows, tokens), F32),
            pltpu.VMEM((n_vocab, tokens, cols), BF16),
            halves, halves,
            pltpu.VMEM((tokens, cols), F32),
            pltpu.VMEM((n_vocab, 8, tokens), F32),
            pltpu.VMEM((n_seq, 8, tokens), jnp.int32),
            pltpu.VMEM((1, tokens), F32),
            dma((2,)), dma,
            dma((3, chips)), dma((3, chips)), dma((3, n_vocab)), dma((3,)),
            dma((n_vocab,)), dma((n_vocab,)), dma((n_seq,)), dma((n_seq,)),
            dma((n_seq,)), dma((n_seq,)), dma((n_seq,)),
            dma((chips,)), dma((chips,)), dma((chips,)), dma((chips,)),
        ],
        compiler_params=pltpu.CompilerParams(
            collective_id=0, has_side_effects=True, vmem_limit_bytes=62 * 1024 * 1024
        ),
        cost_estimate=pl.CostEstimate(
            flops=8 * tokens * vocab_rows * width, bytes_accessed=2 * vocab_rows * width,
            transcendentals=2 * tokens * vocab_rows,
        ),
    )(
        hidden.T, embed_cotangent.T, table,
        jnp.broadcast_to(token_ids[None, :], (8, tokens)),
        target_ids[None, :], loss_scale[None, :],
    )
    return (gh.T, gt.reshape(per * cols, vocab_rows).T, loss[0])


def solution(mesh):
    placed = (P("seq", "vocab"), P("seq", "vocab"), P("vocab", None), P("seq"), P("seq"), P("seq"))
    return jax.shard_map(
        body,
        mesh=mesh,
        in_specs=placed,
        out_specs=(P("seq", "vocab"), P("vocab", "seq"), P("seq")),
        check_vma=False,
    )
```

time: 473 us -> 229 us (0.48)
  waiting for transfers between devices: 372 us -> 0 us
  Pallas kernels: 0 us -> 220 us
  matrix products: 53.4 us -> 0 us
  blocking collectives: 25.3 us -> 0 us
  between operations: 13.8 us -> 0.64 us
  local copies, waits for them, and re-layouts: 0.02 us -> 8.28 us
    reduce_scatter x2 -> x0, waiting for transfers between devices: 326 us -> none  [the longest x1 274 us: body(): lax.psum_scatter(table_term, 'seq', scatter_dimension=1, tiled=True)]
    pallas_call x0 -> x1, Pallas kernels: none -> 220 us  [body(): pl.pallas_call(functools.partial(kernel, n_seq, n_vocab), out_shape=(jax....]
    dot_general x4 -> x0, matrix products: 53.4 us -> none  [the longest x1 18.5 us: body(): lax.dot_general(token_hot, cotangent_full, contract_rows, preferred_eleme...]
    all_gather x2 -> x0, waiting for transfers between devices: 44.7 us -> none  [the longest x1 44.7 us: body(): lax.all_gather(hidden, 'vocab', axis=1, tiled=True)]
    psum x1 -> x0, blocking collectives: 13.6 us -> none  [body(): exp_total, target_logit = lax.psum((local_total, target_local), 'vocab')]
    pmax x1 -> x0, blocking collectives: 11.7 us -> none  [body(): row_top = lax.pmax(jnp.max(logits, axis=1), 'vocab')]
    unnamed x6 -> x5, local copies, waits for them, and re-layouts: 0.02 us -> 7 us
  transfers between devices with their start and end apart: 4 -> 0, of which waited for: 3 -> 0; matrix products, arithmetic and copies ran while one was open for 12% -> 0% of each run, Pallas kernels for 0% -> 0%
where the time goes in v2:
time: 229 us
  Pallas kernels  220 us (96%)
  local copies, waits for them, and re-layouts  8.28 us (4%)
    pallas_call x1, Pallas kernels, body(): pl.pallas_call(functools.partial(kernel, n_seq, n_vocab), out_shape=(jax....  220 us
    unnamed x5, local copies, waits for them, and re-layouts  7 us

profile of v2, /device:TPU:13, one launch (start us, length us, event | category | flops | bytes accessed | tf_op | source)
XLA Modules:
  0.0 229.0 jit_solution(2516798389694492444)
XLA Ops:
  0.6 1.3 broadcast_in_dim.12.ids
  1.9 220.1 %shard_map.85 = (bf16[672,512]{1,0:T(8,128)(2,1)}, f32[2,672,768]{2,1,0:T(8,128)}, f32[1,512]{1,0:T(1,128)}) custom-call(bf16[672,512]{1,0:T(8,128)(2,1)} %bitcast.12, bf16[672,512]{1,0:T(8,128)(2,1)} %bitcast.13, bf16[768,5376]{1,0:T(8,128)(2,1)} %table.1, s32[8,512]{1,0:T(8,128)} %broadcast_in_dim.12.ids, s32[1,512]{1,0:T(1,128)} %bitcast.14, ...), custom_call_target="tpu_custom_call" | custom-call | flops 16911433728 | bytes 8257536 | tf_op jit(solution)/shard_map/pallas_call | solution.py:341
  222.0 2.0 copy.12
  224.0 0.0 copy-start
  224.0 4.4 %copy.13 = f32[768,1344]{0,1:T(8,128)} copy(f32[768,1344]{0,1:T(8,128)} %bitcast.9) | data formatting | bytes 8257536
  228.4 0.0 copy-done
  228.4 0.6 copy.14
Async XLA Ops:
  224.0 4.4 %copy-start = (f32[1,512]{1,0:T(1,128)S(1)}, f32[1,512]{1,0:T(1,128)}, u32[]{:S(2)}) copy-start(f32[1,512]{1,0:T(1,128)} %get-tuple-element.8) | copy-start | bytes 6148

commit v3 on v2

--- a/solution.py
+++ b/solution.py
@@ -22,8 +22,9 @@
     n_seq, n_vocab,
     hid, cot, table, ids, target, scale,
     gh, gt, loss,
-    raw, tab, rows, hcols, ccols, grads, logits, sends, sib, shares, own, stats, ids_all, norm,
-    table_sem, local_sem, push_sem, fwd_sem, block_sem, swap_sem, stat_send, stat_recv, ids_send, ids_recv,
+    raw, tab, rows, hcols, ccols, grads, logits, sends, sib, shares, own, stats, ids_all, norm, stage,
+    table_sem, local_sem, push_sem, fwd_sem, block_sem, half_send, half_recv,
+    stage_send, stage_recv, cross_send, cross_recv, stat_send, stat_recv, ids_send, ids_recv,
     up_sem, down_sem, grads_recv, sib_send, sib_recv, share_send, share_recv,
 ):
     per = n_vocab // n_seq
@@ -33,8 +34,11 @@
     s, v = lax.axis_index("seq"), lax.axis_index("vocab")
     c, k = v // CORES, v % CORES
     twin = c * CORES + (1 - k)
-    swap_to, swap_slot = v // per, s * per + v % per
-    is_self = swap_to == s
+    q, r = v // per, v % per
+    quarter = tokens // n_seq
+    square = chips == 4
+    nx, ny, nd = c + 1 - 2 * (c % 2), (c + 2) % 4, 3 - c
+    half = cols // 2
     base = v * vocab_rows
 
     def remote(src, dst, send, recv, where):
@@ -42,6 +46,9 @@
             src_ref=src, dst_ref=dst, send_sem=send, recv_sem=recv,
             device_id=where, device_id_type=MESH,
         )
+
+    def lanes(b):
+        return pl.ds(pl.multiple_of(b * quarter, quarter), quarter)
 
     def loop(lo, hi, fn):
         lax.fori_loop(lo, hi, lambda i, z: (fn(i), z)[1], 0)
@@ -59,44 +66,86 @@
     loop(1, n_seq, lambda i: pl.semaphore_signal(
         barrier, inc=1, device_id=((s + i) % n_seq, v), device_id_type=MESH))
 
-    @pl.when(jnp.logical_not(is_self))
-    def _():
-        pl.semaphore_signal(barrier, inc=1, device_id=(swap_to, swap_slot), device_id_type=MESH)
-
-    pl.semaphore_wait(barrier, n_vocab + n_seq - 2 + jnp.where(is_self, 0, 1))
+    pl.semaphore_wait(barrier, n_vocab + n_seq - 2)
+
+    def core_of(chip, core):
+        return chip * CORES + core
+
+    def peers(fn):
+        if square:
+            fn(1, nx)
+            fn(2, ny)
+        else:
+            loop(1, chips, lambda i: fn(i, (c + i) % chips))
+
+    def push_copy(a, src, buf, i, u):
+        return remote(src, buf.at[v], push_sem.at[a, i], block_sem.at[a, v], (s, u))
 
     def push(a, src, buf):
-        def one(i):
-            return remote(src, buf.at[v], push_sem.at[a, i], block_sem.at[a, v],
-                          (s, ((c + i) % chips) * CORES + k))
-        loop(1, chips, lambda i: one(i).start())
-        remote(src, buf.at[v], push_sem.at[a, 0], block_sem.at[a, v], (s, twin)).start()
-
-    def push_done(a, src, buf):
-        def one(i):
-            remote(src, buf.at[v], push_sem.at[a, i], block_sem.at[a, v], (s, twin)).wait_send()
-        loop(0, chips, one)
+        peers(lambda i, chip: push_copy(a, src, buf, i, core_of(chip, k)).start())
+        push_copy(a, src, buf, 0, twin).start()
 
     def arrived(a, buf, u):
         remote(buf.at[u], buf.at[u], fwd_sem.at[a, 0], block_sem.at[a, u], (s, twin)).wait_recv()
 
-    def forward(a, buf, i):
-        u = ((c + i) % chips) * CORES + k
+    def forward(a, buf, i, u):
         return remote(buf.at[u], buf.at[u], fwd_sem.at[a, i], block_sem.at[a, u], (s, twin))
 
+    def half_copy(a, buf, i, u, chip):
+        part = buf.at[u, pl.ds(i * half, half), :]
+        return remote(part, part, half_send.at[a, i], half_recv.at[a, i], (s, core_of(chip, k)))
+
+    def near(a, buf):
+        def one(i, chip):
+            u = core_of(chip, k)
+            arrived(a, buf, u)
+            if square:
+                half_copy(a, buf, i - 1, u, ny if i == 1 else nx).start()
+            forward(a, buf, i, u).start()
+        peers(one)
+
+    def far(a, buf):
+        if square:
+            u = core_of(nd, k)
+            half_copy(a, buf, 0, u, ny).wait_recv()
+            half_copy(a, buf, 1, u, nx).wait_recv()
+            forward(a, buf, 3, u).start()
+
+    def from_twin(a, buf):
+        loop(0, chips, lambda i: arrived(a, buf, core_of((c + i) % chips, 1 - k)))
+
+    def gather_done(a, src, buf):
+        peers(lambda i, chip: push_copy(a, src, buf, i, core_of(chip, k)).wait_send())
+        push_copy(a, src, buf, 0, twin).wait_send()
+        loop(1, chips, lambda i: forward(a, buf, i, v).wait_send())
+        if square:
+            half_copy(a, buf, 0, v, ny).wait_send()
+            half_copy(a, buf, 1, v, nx).wait_send()
+
     push(0, hid, rows)
 
-    for a, src, buf in ((1, hid, hcols), (2, cot, ccols)):
-        @pl.when(is_self)
-        def _(a=a, src=src, buf=buf):
-            stay = pltpu.make_async_copy(src, buf.at[v], swap_sem.at[a])
-            stay.start()
-            stay.wait()
-
-        @pl.when(jnp.logical_not(is_self))
-        def _(a=a, src=src, buf=buf):
-            remote(src, buf.at[swap_slot], swap_sem.at[a], block_sem.at[a, swap_slot],
-                   (swap_to, swap_slot)).start()
+    def stage_copy(to):
+        return remote(cot.at[:, lanes(to)], stage.at[q], stage_send.at[to], stage_recv.at[q],
+                      (s, to * per + r))
+    loop(1, n_seq, lambda j: stage_copy((q + j) % n_seq).start())
+    stage[q] = cot[:, lanes(q)]
+
+    def cross(a, j, src, buf):
+        d = (s + j) % n_seq
+        return remote(src(d), buf.at[v, :, lanes(s)], cross_send.at[a, j], cross_recv.at[a, s], (d, v))
+
+    def cross_in(a, buf):
+        def one(j):
+            b = (s + j) % n_seq
+            here = buf.at[v, :, lanes(b)]
+            remote(here, here, cross_send.at[a, j], cross_recv.at[a, b], (b, v)).wait_recv()
+        loop(1, n_seq, one)
+
+    def cot_part(d):
+        return stage.at[d]
+
+    def hid_part(d):
+        return rows.at[d * per + r, :, lanes(q)]
 
     ids_all[s] = ids[...]
 
@@ -116,6 +165,13 @@
             tab[u, at, :] = raw[i % 2, :, u * cols:(u + 1) * cols]
     loop(0, pieces, split)
 
+    def stage_in(j):
+        b = (q + j) % n_seq
+        remote(stage.at[b], stage.at[b], stage_send.at[b], stage_recv.at[b], (s, twin)).wait_recv()
+    loop(1, n_seq, stage_in)
+    loop(1, n_seq, lambda j: cross(1, j, cot_part, ccols).start())
+    ccols[v, :, lanes(s)] = stage[s]
+
     logits[...] = jnp.zeros_like(logits)
     gt[...] = jnp.zeros_like(gt)
     keep.wait()
@@ -123,23 +179,39 @@
     def add_logits(u):
         logits[...] += dot(tab[u], rows[u])
 
-    def logit_step(i):
-        ci = (c + i) % chips
-
-        @pl.when(i > 0)
-        def _():
-            arrived(0, rows, ci * CORES + k)
-            forward(0, rows, i).start()
-        add_logits(ci * CORES + k)
-        arrived(0, rows, ci * CORES + 1 - k)
-        add_logits(ci * CORES + 1 - k)
-    loop(0, chips, logit_step)
-
-    @pl.when(jnp.logical_not(is_self))
-    def _():
-        arrived(1, hcols, v)
-        arrived(2, ccols, v)
-    push(1, hcols.at[v], hcols)
+    add_logits(v)
+    near(0, rows)
+
+    def step(i):
+        chip = (c + i) % chips
+        mine = core_of(chip, k)
+
+        if not square:
+            @pl.when(i > 0)
+            def _():
+                add_logits(mine)
+        arrived(0, rows, core_of(chip, 1 - k))
+        add_logits(core_of(chip, 1 - k))
+    if square:
+        def pair(i):
+            chip = nx * (1 - i) + ny * i
+            add_logits(core_of(chip, k))
+            arrived(0, rows, core_of(chip, 1 - k))
+            add_logits(core_of(chip, 1 - k))
+        loop(0, 2, pair)
+        far(0, rows)
+        add_logits(core_of(nd, k))
+
+    loop(1, n_seq, lambda j: cross(0, j, hid_part, hcols).start())
+    hcols[v, :, lanes(s)] = rows[s * per + r, :, lanes(q)]
+    if square:
+        def last(i):
+            chip = c * (1 - i) + nd * i
+            arrived(0, rows, core_of(chip, 1 - k))
+            add_logits(core_of(chip, 1 - k))
+        loop(0, 2, last)
+    else:
+        loop(0, chips, step)
 
     def piece(i):
         at = pl.ds(pl.multiple_of(i * CHUNK, CHUNK), CHUNK)
@@ -166,6 +238,8 @@
         return remote(stats.at[v], stats.at[v], stat_send.at[i], stat_recv.at[v],
                       (s, (v + i) % n_vocab))
     loop(1, n_vocab, lambda i: stat(i).start())
+    cross_in(1, ccols)
+    push(1, ccols.at[v], ccols)
 
     def stat_wait(i):
         u = (v + i) % n_vocab
@@ -211,6 +285,9 @@
         sends[u] = dot(grads[s], tab[u]).astype(BF16)
         sib_copy(ci).start()
     loop(1, chips + 1, to_twin)
+    near(1, ccols)
+    cross_in(0, hcols)
+    push(2, hcols.at[v], hcols)
 
     def share_copy(ci):
         slot = sends.at[ci * CORES + k]
@@ -228,11 +305,13 @@
             sends[u] = own[...].astype(BF16)
             share_copy(ci).start()
     loop(1, chips + 1, to_chips)
-    push(2, ccols.at[v], ccols)
+
+    def tokens_of(buf, b, j):
+        return jnp.concatenate([buf[i * per + j, :, lanes(b)] for i in range(n_seq)], axis=1)
 
     def add_head(b):
-        def one(r):
-            gt[r] += dot(hcols[b * per + r], grads[b])
+        def one(j):
+            gt[j] += dot(tokens_of(hcols, b, j), grads[b])
         loop(0, per, one)
 
     def take_grads(j):
@@ -263,25 +342,34 @@
         def _():
             add_head(s + j)
 
-    def relay(a, buf):
-        def one(i):
-            arrived(a, buf, ((c + i) % chips) * CORES + k)
-            forward(a, buf, i).start()
-        loop(1, chips, one)
-        loop(0, chips, lambda i: arrived(a, buf, ((c + i) % chips) * CORES + 1 - k))
+    def ids_wait(i):
+        b = (s + i) % n_seq
+        remote(ids, ids_all.at[b], ids_send.at[i], ids_recv.at[b], ((s + i) % n_seq, v)).wait_recv()
+
+    def add_embed(b):
+        entry = base + lax.broadcasted_iota(jnp.int32, (vocab_rows, tokens), 0)
+        hot = jnp.where(entry == ids_all[b][0:1, :], 1.0, 0.0).astype(BF16)
+
+        def one(j):
+            gt[j] += dot(tokens_of(ccols, b, j), hot, (((1,), (1,)), ((), ())))
+        loop(0, per, one)
 
     take_grads(1)
-    relay(1, hcols)
+    far(1, ccols)
+    near(2, hcols)
+    loop(1, n_seq, ids_wait)
+    from_twin(1, ccols)
+    loop(0, n_seq, add_embed)
+    if n_seq > 2:
+        take_grads(2)
+    far(2, hcols)
+    from_twin(2, hcols)
     add_head(s)
     add_heads(1)
     for j in range(2, n_seq):
-        take_grads(j)
+        if j > 2:
+            take_grads(j)
         add_heads(j)
-
-    def ids_wait(i):
-        b = (s + i) % n_seq
-        remote(ids, ids_all.at[b], ids_send.at[i], ids_recv.at[b], ((s + i) % n_seq, v)).wait_recv()
-    loop(1, n_seq, ids_wait)
 
     def share_add(i):
         ci = (c + i) % chips
@@ -291,27 +379,12 @@
     loop(1, chips, share_add)
     gh[...] = own[...].T.astype(BF16)
 
-    relay(2, ccols)
-
-    def add_embed(b):
-        entry = base + lax.broadcasted_iota(jnp.int32, (vocab_rows, tokens), 0)
-        hot = jnp.where(entry == ids_all[b][0:1, :], 1.0, 0.0).astype(BF16)
-
-        def one(r):
-            gt[r] += dot(ccols[b * per + r], hot, (((1,), (1,)), ((), ())))
-        loop(0, per, one)
-    loop(0, n_seq, add_embed)
-
-    push_done(0, hid, rows)
-    push_done(1, hcols.at[v], hcols)
-    push_done(2, ccols.at[v], ccols)
-    for a, buf in ((0, rows), (1, hcols), (2, ccols)):
-        loop(1, chips, lambda i, a=a, buf=buf: forward(a, buf, i).wait_send())
-    for a, src, buf in ((1, hid, hcols), (2, cot, ccols)):
-        @pl.when(jnp.logical_not(is_self))
-        def _(a=a, src=src, buf=buf):
-            remote(src, buf.at[swap_slot], swap_sem.at[a], block_sem.at[a, swap_slot],
-                   (swap_to, swap_slot)).wait_send()
+    gather_done(0, hid, rows)
+    gather_done(1, ccols.at[v], ccols)
+    gather_done(2, hcols.at[v], hcols)
+    loop(1, n_seq, lambda j: stage_copy((q + j) % n_seq).wait_send())
+    loop(1, n_seq, lambda j: cross(0, j, hid_part, hcols).wait_send())
+    loop(1, n_seq, lambda j: cross(1, j, cot_part, ccols).wait_send())
 
     def ids_left(i):
         remote(ids, ids_all.at[s], ids_send.at[i], ids_recv.at[s], ((s + i) % n_seq, v)).wait_send()
@@ -359,8 +432,10 @@
             pltpu.VMEM((n_vocab, 8, tokens), F32),
             pltpu.VMEM((n_seq, 8, tokens), jnp.int32),
             pltpu.VMEM((1, tokens), F32),
+            pltpu.VMEM((n_seq, cols, tokens // n_seq), BF16),
             dma((2,)), dma,
-            dma((3, chips)), dma((3, chips)), dma((3, n_vocab)), dma((3,)),
+            dma((3, chips)), dma((3, chips)), dma((3, n_vocab)), dma((3, 2)), dma((3, 2)),
+            dma((n_seq,)), dma((n_seq,)), dma((2, n_seq)), dma((2, n_seq)),
             dma((n_vocab,)), dma((n_vocab,)), dma((n_seq,)), dma((n_seq,)),
             dma((n_seq,)), dma((n_seq,)), dma((n_seq,)),
             dma((chips,)), dma((chips,)), dma((chips,)), dma((chips,)),

time: 229 us -> 153 us (0.67)
  Pallas kernels: 220 us -> 144 us
    pallas_call x1, Pallas kernels: 220 us -> 144 us  [body(): pl.pallas_call(functools.partial(kernel, n_seq, n_vocab), out_shape=(jax....]
where the time goes in v3:
time: 153 us
  Pallas kernels  144 us (94%)
  local copies, waits for them, and re-layouts  8.28 us (5%)
    pallas_call x1, Pallas kernels, body(): pl.pallas_call(functools.partial(kernel, n_seq, n_vocab), out_shape=(jax....  144 us
    unnamed x5, local copies, waits for them, and re-layouts  7 us

profile of v3, /device:TPU:13, one launch (start us, length us, event | category | flops | bytes accessed | tf_op | source)
XLA Modules:
  0.0 152.7 jit_solution(445962392026959830)
XLA Ops:
  0.6 1.3 broadcast_in_dim.12.ids
  1.9 143.8 %shard_map.85 = (bf16[672,512]{1,0:T(8,128)(2,1)}, f32[2,672,768]{2,1,0:T(8,128)}, f32[1,512]{1,0:T(1,128)}) custom-call(bf16[672,512]{1,0:T(8,128)(2,1)} %bitcast.12, bf16[672,512]{1,0:T(8,128)(2,1)} %bitcast.13, bf16[768,5376]{1,0:T(8,128)(2,1)} %table.1, s32[8,512]{1,0:T(8,128)} %broadcast_in_dim.12.ids, s32[1,512]{1,0:T(1,128)} %bitcast.14, ...), custom_call_target="tpu_custom_call" | custom-call | flops 16911433728 | bytes 8257536 | tf_op jit(solution)/shard_map/pallas_call | solution.py:414
  145.7 2.0 %copy.12 = bf16[512,672]{0,1:T(8,128)(2,1)} copy(bf16[512,672]{0,1:T(8,128)(2,1)} %bitcast.10) | data formatting | bytes 1376256
  147.7 0.0 copy-start
  147.7 4.4 %copy.13 = f32[768,1344]{0,1:T(8,128)} copy(f32[768,1344]{0,1:T(8,128)} %bitcast.9) | data formatting | bytes 8257536
  152.1 0.0 copy-done
  152.1 0.6 copy.14
Async XLA Ops:
  147.7 4.4 %copy-start = (f32[1,512]{1,0:T(1,128)S(1)}, f32[1,512]{1,0:T(1,128)}, u32[]{:S(2)}) copy-start(f32[1,512]{1,0:T(1,128)} %get-tuple-element.8) | copy-start | bytes 6148

commit v4 on v3

--- a/solution.py
+++ b/solution.py
@@ -22,10 +22,11 @@
     n_seq, n_vocab,
     hid, cot, table, ids, target, scale,
     gh, gt, loss,
-    raw, tab, rows, hcols, ccols, grads, logits, sends, sib, shares, own, stats, ids_all, norm, stage,
+    raw, tab, rows, hcols, ccols, grads, logits, sends, sib, shares, own, stats, ids_all, norm, stage, corner,
     table_sem, local_sem, push_sem, fwd_sem, block_sem, half_send, half_recv,
     stage_send, stage_recv, cross_send, cross_recv, stat_send, stat_recv, ids_send, ids_recv,
     up_sem, down_sem, grads_recv, sib_send, sib_recv, share_send, share_recv,
+    corner_send, corner_recv, side_send, side_recv,
 ):
     per = n_vocab // n_seq
     chips = n_vocab // CORES
@@ -147,10 +148,14 @@
     def hid_part(d):
         return rows.at[d * per + r, :, lanes(q)]
 
-    ids_all[s] = ids[...]
+    ids_all[s] = jnp.broadcast_to(ids[...], (8, tokens))
+
+    def ids_copy(i):
+        mine = ids_all.at[s]
+        return remote(mine, mine, ids_send.at[i], ids_recv.at[s], ((s + i) % n_seq, v))
 
     def send_ids(i):
-        remote(ids, ids_all.at[s], ids_send.at[i], ids_recv.at[s], ((s + i) % n_seq, v)).start()
+        ids_copy(i).start()
     loop(1, n_seq, send_ids)
 
     pieces = vocab_rows // CHUNK
@@ -204,6 +209,8 @@
 
     loop(1, n_seq, lambda j: cross(0, j, hid_part, hcols).start())
     hcols[v, :, lanes(s)] = rows[s * per + r, :, lanes(q)]
+    cross_in(1, ccols)
+    push(1, ccols.at[v], ccols)
     if square:
         def last(i):
             chip = c * (1 - i) + nd * i
@@ -238,8 +245,6 @@
         return remote(stats.at[v], stats.at[v], stat_send.at[i], stat_recv.at[v],
                       (s, (v + i) % n_vocab))
     loop(1, n_vocab, lambda i: stat(i).start())
-    cross_in(1, ccols)
-    push(1, ccols.at[v], ccols)
 
     def stat_wait(i):
         u = (v + i) % n_vocab
@@ -293,18 +298,67 @@
         slot = sends.at[ci * CORES + k]
         return remote(slot, shares.at[c], share_send.at[ci], share_recv.at[c], (s, ci * CORES + k))
 
+    def pair_sum(ci):
+        own[...] = dot(grads[s], tab[ci * CORES + k])
+        sib_copy(ci).wait_recv()
+        own[...] += sib[ci].astype(F32)
+
     def to_chips(i):
         ci = (c + i) % chips
-        u = ci * CORES + k
-        own[...] = dot(grads[s], tab[u])
-        sib_copy(ci).wait_recv()
-        own[...] += sib[ci].astype(F32)
+        pair_sum(ci)
 
         @pl.when(i < chips)
         def _():
-            sends[u] = own[...].astype(BF16)
+            sends[ci * CORES + k] = own[...].astype(BF16)
             share_copy(ci).start()
-    loop(1, chips + 1, to_chips)
+
+    side = tokens // 2
+
+    def side_of(i):
+        return pl.ds(i * side, side)
+
+    def corner_copy(i):
+        return remote(sends.at[nd * CORES + k, side_of(i), :], corner.at[i], corner_send.at[i],
+                      corner_recv.at[i], (s, (ny if i else nx) * CORES + k))
+
+    def side_copy(to, i):
+        chip = ny if to else nx
+        return remote(sends.at[chip * CORES + k, side_of(i), :], shares.at[c, side_of(i), :],
+                      side_send.at[to, i], side_recv.at[to, i], (s, chip * CORES + k))
+
+    def share_start():
+        if not square:
+            loop(1, chips + 1, to_chips)
+            return
+
+        def one(i):
+            ci = c + (i == 0) * (nd - c) + (i == 1) * (nx - c) + (i == 2) * (ny - c)
+            pair_sum(ci)
+
+            @pl.when(i < 3)
+            def _():
+                sends[ci * CORES + k] = own[...].astype(BF16)
+            for at, copies in enumerate(
+                ((corner_copy(0), corner_copy(1)), (side_copy(0, 0),), (side_copy(1, 1),))
+            ):
+                @pl.when(i == at)
+                def _(copies=copies):
+                    for copy in copies:
+                        copy.start()
+        loop(0, 4, one)
+
+    def share_pass():
+        if square:
+            for to in (0, 1):
+                corner_copy(1 - to).wait_recv()
+                u = (ny if to else nx) * CORES + k
+                at = side_of(1 - to)
+                sends[u, at, :] = (
+                    sends[u, at, :].astype(F32) + corner[1 - to].astype(F32)
+                ).astype(BF16)
+                side_copy(to, 1 - to).start()
+
+    share_start()
 
     def tokens_of(buf, b, j):
         return jnp.concatenate([buf[i * per + j, :, lanes(b)] for i in range(n_seq)], axis=1)
@@ -344,7 +398,7 @@
 
     def ids_wait(i):
         b = (s + i) % n_seq
-        remote(ids, ids_all.at[b], ids_send.at[i], ids_recv.at[b], ((s + i) % n_seq, v)).wait_recv()
+        remote(ids_all.at[b], ids_all.at[b], ids_send.at[i], ids_recv.at[b], (b, v)).wait_recv()
 
     def add_embed(b):
         entry = base + lax.broadcasted_iota(jnp.int32, (vocab_rows, tokens), 0)
@@ -357,6 +411,7 @@
     take_grads(1)
     far(1, ccols)
     near(2, hcols)
+    share_pass()
     loop(1, n_seq, ids_wait)
     from_twin(1, ccols)
     loop(0, n_seq, add_embed)
@@ -371,12 +426,21 @@
             take_grads(j)
         add_heads(j)
 
-    def share_add(i):
+    def share_add(ci):
+        own[...] += shares[ci].astype(F32)
+
+    def share_in(i):
         ci = (c + i) % chips
         remote(shares.at[ci], shares.at[ci], share_send.at[ci], share_recv.at[ci],
                (s, twin)).wait_recv()
-        own[...] += shares[ci].astype(F32)
-    loop(1, chips, share_add)
+        share_add(ci)
+    if square:
+        for to in (0, 1):
+            side_copy(to, 0).wait_recv()
+            side_copy(to, 1).wait_recv()
+            share_add(ny if to else nx)
+    else:
+        loop(1, chips, share_in)
     gh[...] = own[...].T.astype(BF16)
 
     gather_done(0, hid, rows)
@@ -387,11 +451,17 @@
     loop(1, n_seq, lambda j: cross(1, j, cot_part, ccols).wait_send())
 
     def ids_left(i):
-        remote(ids, ids_all.at[s], ids_send.at[i], ids_recv.at[s], ((s + i) % n_seq, v)).wait_send()
+        ids_copy(i).wait_send()
     loop(1, n_seq, ids_left)
     loop(1, n_vocab, lambda i: stat(i).wait_send())
     loop(0, chips, lambda i: sib_copy(i).wait_send())
-    loop(1, chips, lambda i: share_copy((c + i) % chips).wait_send())
+    if square:
+        for i in (0, 1):
+            corner_copy(i).wait_send()
+            side_copy(0, i).wait_send()
+            side_copy(1, i).wait_send()
+    else:
+        loop(1, chips, lambda i: share_copy((c + i) % chips).wait_send())
     for b in range(n_seq):
         @pl.when(jnp.logical_and(s >= b, s < n_seq - 1))
         def _(b=b):
@@ -433,12 +503,14 @@
             pltpu.VMEM((n_seq, 8, tokens), jnp.int32),
             pltpu.VMEM((1, tokens), F32),
             pltpu.VMEM((n_seq, cols, tokens // n_seq), BF16),
+            pltpu.VMEM((2, tokens // 2, cols), BF16),
             dma((2,)), dma,
             dma((3, chips)), dma((3, chips)), dma((3, n_vocab)), dma((3, 2)), dma((3, 2)),
             dma((n_seq,)), dma((n_seq,)), dma((2, n_seq)), dma((2, n_seq)),
             dma((n_vocab,)), dma((n_vocab,)), dma((n_seq,)), dma((n_seq,)),
             dma((n_seq,)), dma((n_seq,)), dma((n_seq,)),
             dma((chips,)), dma((chips,)), dma((chips,)), dma((chips,)),
+            dma((2,)), dma((2,)), dma((2, 2)), dma((2, 2)),
         ],
         compiler_params=pltpu.CompilerParams(
             collective_id=0, has_side_effects=True, vmem_limit_bytes=62 * 1024 * 1024
@@ -449,8 +521,7 @@
         ),
     )(
         hidden.T, embed_cotangent.T, table,
-        jnp.broadcast_to(token_ids[None, :], (8, tokens)),
-        target_ids[None, :], loss_scale[None, :],
+        token_ids[None, :], target_ids[None, :], loss_scale[None, :],
     )
     return (gh.T, gt.reshape(per * cols, vocab_rows).T, loss[0])
 

time: 153 us -> 147 us (0.961)
  the two profiles are of different devices: /device:TPU:13 before, /device:TPU:0 now
where the time goes in v4:
time: 147 us
  Pallas kernels  139 us (95%)
  local copies, waits for them, and re-layouts  7 us (5%)
    pallas_call x1, Pallas kernels, body(): pl.pallas_call(functools.partial(kernel, n_seq, n_vocab), out_shape=(jax....  139 us
    unnamed x5, local copies, waits for them, and re-layouts  7 us

profile of v4, /device:TPU:0, one launch (start us, length us, event | category | flops | bytes accessed | tf_op | source)
XLA Modules:
  0.0 146.9 jit_solution(10730330639860888611)
XLA Ops:
  0.6 139.2 %shard_map.85 = (bf16[672,512]{1,0:T(8,128)(2,1)}, f32[2,672,768]{2,1,0:T(8,128)}, f32[1,512]{1,0:T(1,128)}) custom-call(bf16[672,512]{1,0:T(8,128)(2,1)} %bitcast.13, bf16[672,512]{1,0:T(8,128)(2,1)} %bitcast.14, bf16[768,5376]{1,0:T(8,128)(2,1)} %table.1, s32[1,512]{1,0:T(1,128)} %bitcast.15, s32[1,512]{1,0:T(1,128)} %bitcast.16, f32[1,512]{1,0:T(1,128)} %bitcast.17), custom_call_target="tpu_custom_call" | custom-call | flops 16911433728 | bytes 8257536 | tf_op jit(solution)/shard_map/pallas_call | solution.py:484
  139.9 2.0 %copy.12 = bf16[512,672]{0,1:T(8,128)(2,1)} copy(bf16[512,672]{0,1:T(8,128)(2,1)} %bitcast.11) | data formatting | bytes 1376256
  141.9 0.0 copy-start
  141.9 4.4 %copy.13 = f32[768,1344]{0,1:T(8,128)} copy(f32[768,1344]{0,1:T(8,128)} %bitcast.10) | data formatting | bytes 8257536
  146.3 0.0 copy-done
  146.3 0.6 copy.14
Async XLA Ops:
  141.9 4.4 %copy-start = (f32[1,512]{1,0:T(1,128)S(1)}, f32[1,512]{1,0:T(1,128)}, u32[]{:S(2)}) copy-start(f32[1,512]{1,0:T(1,128)} %get-tuple-element.8) | copy-start | bytes 6148

commit v5 on v4

--- a/solution.py
+++ b/solution.py
@@ -170,22 +170,22 @@
             tab[u, at, :] = raw[i % 2, :, u * cols:(u + 1) * cols]
     loop(0, pieces, split)
 
+    logits[...] = jnp.zeros_like(logits)
+    gt[...] = jnp.zeros_like(gt)
+    keep.wait()
+
+    def add_logits(u):
+        logits[...] += dot(tab[u], rows[u])
+
+    add_logits(v)
+    near(0, rows)
+
     def stage_in(j):
         b = (q + j) % n_seq
         remote(stage.at[b], stage.at[b], stage_send.at[b], stage_recv.at[b], (s, twin)).wait_recv()
     loop(1, n_seq, stage_in)
     loop(1, n_seq, lambda j: cross(1, j, cot_part, ccols).start())
     ccols[v, :, lanes(s)] = stage[s]
-
-    logits[...] = jnp.zeros_like(logits)
-    gt[...] = jnp.zeros_like(gt)
-    keep.wait()
-
-    def add_logits(u):
-        logits[...] += dot(tab[u], rows[u])
-
-    add_logits(v)
-    near(0, rows)
 
     def step(i):
         chip = (c + i) % chips
@@ -284,6 +284,9 @@
         slot = sends.at[ci * CORES + 1 - k]
         return remote(slot, sib.at[ci], sib_send.at[ci], sib_recv.at[ci], (s, twin))
 
+    cross_in(0, hcols)
+    push(2, hcols.at[v], hcols)
+
     def to_twin(i):
         ci = (c + i) % chips
         u = ci * CORES + 1 - k
@@ -291,8 +294,6 @@
         sib_copy(ci).start()
     loop(1, chips + 1, to_twin)
     near(1, ccols)
-    cross_in(0, hcols)
-    push(2, hcols.at[v], hcols)
 
     def share_copy(ci):
         slot = sends.at[ci * CORES + k]
@@ -409,15 +410,15 @@
         loop(0, per, one)
 
     take_grads(1)
+    near(2, hcols)
     far(1, ccols)
-    near(2, hcols)
+    if n_seq > 2:
+        take_grads(2)
     share_pass()
+    far(2, hcols)
     loop(1, n_seq, ids_wait)
     from_twin(1, ccols)
     loop(0, n_seq, add_embed)
-    if n_seq > 2:
-        take_grads(2)
-    far(2, hcols)
     from_twin(2, hcols)
     add_head(s)
     add_heads(1)

time: 147 us -> 144 us (0.980)
  the two profiles are of different devices: /device:TPU:0 before, /device:TPU:13 now
where the time goes in v5:
time: 144 us; the launch traced here: 142 us
  Pallas kernels  135 us (94%)
  local copies, waits for them, and re-layouts  7 us (5%)
    pallas_call x1, Pallas kernels, body(): pl.pallas_call(functools.partial(kernel, n_seq, n_vocab), out_shape=(jax....  135 us
    unnamed x5, local copies, waits for them, and re-layouts  7 us

profile of v5, /device:TPU:13, one launch (start us, length us, event | category | flops | bytes accessed | tf_op | source)
XLA Modules:
  0.0 142.2 jit_solution(12888477165244091967)
XLA Ops:
  0.6 134.6 %shard_map.85 = (bf16[672,512]{1,0:T(8,128)(2,1)}, f32[2,672,768]{2,1,0:T(8,128)}, f32[1,512]{1,0:T(1,128)}) custom-call(bf16[672,512]{1,0:T(8,128)(2,1)} %bitcast.13, bf16[672,512]{1,0:T(8,128)(2,1)} %bitcast.14, bf16[768,5376]{1,0:T(8,128)(2,1)} %table.1, s32[1,512]{1,0:T(1,128)} %bitcast.15, s32[1,512]{1,0:T(1,128)} %bitcast.16, f32[1,512]{1,0:T(1,128)} %bitcast.17), custom_call_target="tpu_custom_call" | custom-call | flops 16911433728 | bytes 8257536 | tf_op jit(solution)/shard_map/pallas_call | solution.py:485
  135.2 2.0 %copy.12 = bf16[512,672]{0,1:T(8,128)(2,1)} copy(bf16[512,672]{0,1:T(8,128)(2,1)} %bitcast.11) | data formatting | bytes 1376256
  137.2 0.0 copy-start
  137.2 4.4 %copy.13 = f32[768,1344]{0,1:T(8,128)} copy(f32[768,1344]{0,1:T(8,128)} %bitcast.10) | data formatting | bytes 8257536
  141.6 0.0 copy-done
  141.6 0.6 copy.14
Async XLA Ops:
  137.2 4.4 %copy-start = (f32[1,512]{1,0:T(1,128)S(1)}, f32[1,512]{1,0:T(1,128)}, u32[]{:S(2)}) copy-start(f32[1,512]{1,0:T(1,128)} %get-tuple-element.8) | copy-start | bytes 6148
